TPU v7x, 256 devices: a whole 4x4x8 slice. The times are simulated.
256 devices in a mesh: pos: 128 (over y, z, x), pix: 2 (over core).
Axes of the slice: x: 4, y: 4, z: 8, core: 2. Of those that a mesh axis runs over, the one named last changes fastest.
Arguments:
- frames: float32 [8192, 128, 128], P('pos', None, 'pix'), may hold values from -96 to 96
- sketch: bfloat16 [128, 128, 256], P(None, 'pix'), may hold values from -0.046875 to 0.046875
Outputs:
- denoised: float32 [128, 128, 8192], P('pos', 'pix')
All inputs are finite; a program needn't handle non-finite values.
Results may differ from a plain program's by a relative error of at most 0.0037.
Values sent between devices are 32-bit elements; how exact they have to be, the bound alone decides.
A program may use at most 128 MiB of HBM per device.

v0:
```python
import jax
import jax.numpy as jnp
from jax import lax
from jax.sharding import PartitionSpec as P


def body(frames, sketch):
    frame_count = frames.shape[0]
    local_rows = frames.shape[1]
    local_cols = frames.shape[2]
    pixel_count = local_rows * local_cols
    flat_frames = frames.reshape(frame_count, pixel_count)
    test_matrix = sketch.reshape(pixel_count, sketch.shape[2])
    partial_sketch = jnp.dot(
        flat_frames.astype(jnp.bfloat16), test_matrix, preferred_element_type=jnp.float32
    )
    sketched = lax.psum(partial_sketch, "pix")
    gram_part = jnp.dot(
        sketched.T, sketched, precision=lax.Precision.HIGHEST, preferred_element_type=jnp.float32
    )
    gram = lax.psum(gram_part, "pos")
    factor = jnp.linalg.cholesky(gram)
    basis_t = lax.linalg.triangular_solve(factor, sketched.T, left_side=True, lower=True)
    my_coeffs = lax.psum_scatter(
        lax.dot_general(
            flat_frames,
            basis_t,
            (((0,), (1,)), ((), ())),
            precision=lax.Precision.HIGHEST,
            preferred_element_type=jnp.float32,
        ),
        "pos",
        scatter_dimension=0,
        tiled=True,
    )
    rebuilt = jnp.dot(
        lax.all_gather(my_coeffs, "pos", axis=0, tiled=True),
        basis_t,
        precision=lax.Precision.HIGHEST,
        preferred_element_type=jnp.float32,
    )
    rebuilt = rebuilt.reshape(local_rows, local_cols, frame_count)
    return lax.all_to_all(rebuilt, "pos", split_axis=0, concat_axis=2, tiled=True)


def solution(mesh):
    in_specs = (P("pos", None, "pix"), P(None, "pix", None))
    out_specs = P("pos", "pix", None)
    return jax.shard_map(body, mesh=mesh, in_specs=in_specs, out_specs=out_specs, check_vma=False)
```

profile of v0, /device:TPU:3, one launch (start us, length us, event | category | flops | bytes accessed | tf_op | source)
XLA Modules:
  0.0 1287.0 jit_solution(3649650825656216395)
XLA Ops:
  6.5 0.0 all-reduce.4.cloned.1.call-start
  6.5 1.8 convert_element_type.4
  8.3 3.7 copy.14
  12.0 0.0 copy-start
  12.0 4.4 convolution_bitcast_fusion.1
  16.5 0.0 all-reduce.4.cloned.1.call-update
  16.5 0.0 all-reduce.6.cloned.1.call-start
  16.5 32.0 %all-reduce.4.cloned.1.call-done = f32[64,256]{1,0:T(8,128)} async-done(((f32[64,256]{1,0:T(8,128)}), f32[64,256]{1,0:T(8,128)}) %all-reduce.4.cloned.1.call-update) | async-done | bytes 65552 | tf_op jit(solution)/shard_map/psum | solution.py:17
  48.5 2.0 fusion.12
  50.6 0.0 all-reduce.6.cloned.1.call-update
  50.6 0.4 reduce-scatter.4.cloned.1.call-start
  51.0 0.0 copy-done
  51.1 2.7 copy.17
  53.7 0.0 copy-start.1
  53.8 3.5 reshape.25
  57.3 205.9 %all-reduce.6.cloned.1.call-done = f32[256,256]{0,1:T(8,128)} async-done(((f32[256,256]{0,1:T(8,128)}), f32[256,256]{0,1:T(8,128)}) %all-reduce.6.cloned.1.call-update) | async-done | bytes 262160 | tf_op jit(solution)/shard_map/psum | solution.py:21
  263.2 1.1 copy.16
  264.3 1.0 fusion
  265.3 11.7 cholesky.50
  277.1 9.8 custom-call.14
  286.9 0.2 constant_dynamic-update-slice_fusion.1
  287.1 0.3 convolution_subtract_fusion
  287.4 11.7 cholesky.105
  299.1 0.7 compare_reduce_fusion
  301.2 0.1 triangular_solve.57
  301.3 4.1 while.1
  301.3 0.6 fusion.24
  301.9 1.4 bitcast_dynamic-update-slice_fusion.2
  303.4 0.6 fusion.24
  304.0 1.4 bitcast_dynamic-update-slice_fusion.2
  305.4 30.7 %custom-call.15 = f32[2,128,128]{1,2,0:T(8,128)S(1)} custom-call(f32[2,128,128]{2,1,0:T(8,128)S(1)} %get-tuple-element.12), custom_call_target="InvertDiagBlocksLowerTriangular" | custom-call | tf_op jit(solution)/shard_map/triangular_solve | solution.py:23
  336.1 0.0 copy-done.1
  336.1 0.2 fusion.3
  336.3 0.2 convolution_subtract_fusion.1
  336.5 0.2 fusion.2
  336.7 8.9 convolution_bitcast_fusion
  345.6 9.0 copy.23
  354.6 0.0 reduce-scatter.4.cloned.1.call-update
  354.7 0.0 all-gather.2.cloned.1.call-start
  354.7 606.0 %reduce-scatter.4.cloned.1.call-done = f32[64,256]{1,0:T(8,128)} async-done(((f32[8192,256]{1,0:T(8,128)}), f32[64,256]{1,0:T(8,128)}) %reduce-scatter.4.cloned.1.call-update) | async-done | bytes 65552 | tf_op jit(solution)/shard_map/reduce_scatter | solution.py:24
  960.7 0.0 all-gather.2.cloned.1.call-update
  960.8 224.0 %all-gather.2.cloned.1.call-done = f32[8192,256]{1,0:T(8,128)} async-done(((f32[64,256]{1,0:T(8,128)}), f32[8192,256]{1,0:T(8,128)}) %all-gather.2.cloned.1.call-update) | async-done | bytes 8388624 | tf_op jit(solution)/shard_map/all_gather | solution.py:37
  1184.7 10.5 fusion.7
  1195.2 3.0 reshape.26
  1198.2 6.6 copy.26
  1204.8 4.6 reshape.49
  1209.4 56.3 %all_to_all.18 = f32[128,1,4096]{2,1,0:T(1,128)} all-to-all(f32[128,1,4096]{2,1,0:T(1,128)S(1)} %reshape.49), channel_id=1, replica_groups=mesh['pos'=128,'pix'=2] {'pos'}, dimensions={0} | all-to-all | bytes 4194304 | tf_op jit(solution)/shard_map/all_to_all | solution.py:43
  1265.7 0.5 broadcast.107
  1266.2 7.3 reduce.12
  1273.5 3.0 reshape.50
  1276.5 3.8 copy.22
  (9 shorter events, 0.1 us)
Async XLA Ops:
  6.5 42.0 %all-reduce.4.cloned.1.call-start = ((), (), s32[]{:S(2)}) async-start(), calls=%async_computation.2 | async-start | bytes 131072 | tf_op jit(solution)/shard_map/psum | solution.py:17
  12.0 39.0 %copy-start = (f32[64,128,64]{1,2,0:T(8,128)S(1)}, f32[64,128,64]{1,2,0:T(8,128)}, u32[]{:S(2)}) copy-start(f32[64,128,64]{1,2,0:T(8,128)} %param.2) | copy-start | bytes 6291460
  16.5 246.7 %all-reduce.6.cloned.1.call-start = ((), (), s32[]{:S(2)}) async-start(), calls=%async_computation.3 | async-start | bytes 524288 | tf_op jit(solution)/shard_map/psum | solution.py:21
  50.6 910.1 %reduce-scatter.4.cloned.1.call-start = ((), (), s32[]{:S(2)}) async-start(), calls=%async_computation.5 | async-start | bytes 8454144 | tf_op jit(solution)/shard_map/reduce_scatter | solution.py:24
  53.7 282.3 %copy-start.1 = (f32[64,256]{1,0:T(8,128)S(1)}, f32[64,256]{1,0:T(8,128)}, u32[]{:S(2)}) copy-start(f32[64,256]{1,0:T(8,128)} %all-reduce.4.cloned.1.call-done) | copy-start | bytes 196612
  354.7 830.1 %all-gather.2.cloned.1.call-start = ((), (), s32[]{:S(2)}) async-start(), calls=%async_computation.4 | async-start | bytes 8454144 | tf_op jit(solution)/shard_map/all_gather | solution.py:37
Sparse Core Ops, SparseCore 0:
  16.6 31.8 all-reduce.3
  54.0 209.2 all-reduce.5
  354.8 605.9 reduce-scatter.3
  964.2 220.4 all-gather.1
where the time goes:
time: 1300 us; the launch traced here: 1290 us
  waiting for transfers between devices  1070 us (82%)
  other arithmetic  74.8 us (6%)
  blocking collectives  56.3 us (4%)
  local copies, waits for them, and re-layouts  45.6 us (4%)
  matrix products  27 us (2%)
  between operations  14.9 us (1%)
    reduce_scatter x1, waiting for transfers between devices, body(): lax.psum_scatter(lax.dot_general(flat_frames, basis_t, (((0,), (1,)), (()...  606 us
    all_gather x1, waiting for transfers between devices, body(): lax.all_gather(my_coeffs, 'pos', axis=0, tiled=True)  224 us
    psum x1, waiting for transfers between devices, body(): gram = lax.psum(gram_part, 'pos')  206 us
    all_to_all x1, blocking collectives, body(): lax.all_to_all(rebuilt, 'pos', split_axis=0, concat_axis=2, tiled=True)  56.3 us
    another operation x6, other arithmetic, body(): factor = jnp.linalg.cholesky(gram)  34 us
    psum x1, waiting for transfers between devices, body(): sketched = lax.psum(partial_sketch, 'pix')  32 us
    another operation x3, other arithmetic, body(): lax.linalg.triangular_solve(factor, sketched.T, left_side=True, lower=True)  30.7 us
  transfers between devices with their start and end apart: 4, of which 4 were waited for; matrix products, arithmetic and copies ran while one was open for 0% of the time, Pallas kernels for 0%

commit v1 on v0

v1 whole, which is shorter than its diff:
```python
import jax
import jax.numpy as jnp
from jax import lax
from jax.experimental import pallas as pl
from jax.experimental.pallas import tpu as pltpu
from jax.sharding import PartitionSpec as P

MESH = pl.DeviceIdType.MESH
HIGHEST = lax.Precision.HIGHEST
NY, NZ, NX = 4, 8, 4
PLANE = NY * NX
RANK = 256
BLOCK, PANEL = 8, 32
TIES = [k for k in range(1, PLANE) if k // NX == 2 or k % NX == 2]
EARLY = [1, 3]
LATE = [k for k in range(1, PLANE) if k not in TIES + EARLY]


def tn(a, b, precision=None):
    return lax.dot_general(a, b, (((0,), (0,)), ((), ())), precision=precision, preferred_element_type=jnp.float32)


def nt(a, b, precision=None):
    return lax.dot_general(a, b, (((1,), (1,)), ((), ())), precision=precision, preferred_element_type=jnp.float32)


def nn(a, b, precision=None):
    return jnp.dot(a, b, precision=precision, preferred_element_type=jnp.float32)


def halves(a):
    high = a.astype(jnp.bfloat16)
    return high, (a - high.astype(jnp.float32)).astype(jnp.bfloat16)


def splat(rows, i):
    return jnp.broadcast_to(rows[:, i : i + 1], (BLOCK, 128))


def lanes_of(rows, base):
    tile = jnp.where(base < 128, rows[:, 0:128], rows[:, 128:256])
    return pltpu.roll(tile, lax.rem(256 - base, 128), 1)


def factor_diagonal(a):
    groups = [a[g * BLOCK : (g + 1) * BLOCK] for g in range(PANEL // BLOCK)]
    sub = lax.broadcasted_iota(jnp.int32, (BLOCK, 128), 0)
    for q in range(PANEL // BLOCK):
        rows = [jnp.broadcast_to(groups[q][k : k + 1, :], (BLOCK, 128)) for k in range(BLOCK)]
        columns = [[splat(groups[g], q * BLOCK + k) for k in range(BLOCK)] for g in range(q + 1, PANEL // BLOCK)]
        s = [[splat(rows[i], q * BLOCK + k) for k in range(i + 1)] for i in range(BLOCK)]
        inv, done = [], []
        for k in range(BLOCK):
            inv.append(lax.rsqrt(s[k][k]))
            for i in range(k + 1, BLOCK):
                s[i][k] = s[i][k] * inv[k]
            for i in range(k + 1, BLOCK):
                for m in range(k + 1, i + 1):
                    s[i][m] = s[i][m] - s[i][k] * s[m][k]
            row = rows[k]
            for i in range(k):
                row = row - s[k][i] * done[i]
            done.append(row * inv[k])
        for g in range(q + 1, PANEL // BLOCK):
            times = []
            for k in range(BLOCK):
                t = columns[g - q - 1][k]
                for i in range(k):
                    t = t - times[i] * s[k][i]
                times.append(t * inv[k])
                groups[g] = groups[g] - times[k] * done[k]
        block = done[0]
        for k in range(1, BLOCK):
            block = jnp.where(sub == k, done[k], block)
        groups[q] = block
    return jnp.concatenate(groups, axis=0)


def factor_step(o, last, a_ref):
    base = pl.multiple_of(o * PANEL, PANEL)
    lane = lax.broadcasted_iota(jnp.int32, (1, RANK), 1)
    before = (lane >= base - PANEL) & (lane < base)
    rows = jnp.where(before, 0.0, a_ref[pl.ds(base, PANEL), :])
    rows = rows - tn(lanes_of(last, base)[:, 0:PANEL], last, HIGHEST)
    row_at = lax.broadcasted_iota(jnp.int32, (PANEL, 128), 0)
    lane_at = lax.broadcasted_iota(jnp.int32, (PANEL, 128), 1)
    both = jnp.where(lane_at < PANEL, lanes_of(rows, base), jnp.where(lane_at == row_at + PANEL, 1.0, 0.0))
    both = factor_diagonal(both)
    inverse = jnp.where((lane_at >= PANEL) & (lane_at < 2 * PANEL), both, 0.0)
    own = (lane >= base) & (lane < base + PANEL)
    unit = lane == base + lax.broadcasted_iota(jnp.int32, (PANEL, 1), 0)
    rows = jnp.where(own, jnp.where(unit, 1.0, 0.0), rows)
    zeros = jnp.zeros((PANEL, RANK), jnp.float32)
    panel = nn(inverse, jnp.concatenate([zeros, rows, zeros, zeros], axis=0), HIGHEST)
    right = jnp.where(lane >= base, last, 0.0)
    below = lax.broadcasted_iota(jnp.int32, (RANK, 1), 0) >= base
    a_ref[...] = jnp.where(below & before, 0.0, a_ref[...]) - tn(right, last, HIGHEST)

    @pl.when(o > 0)
    def _():
        a_ref[pl.ds(pl.multiple_of(jnp.maximum(base - PANEL, 0), PANEL), PANEL), :] = last

    return panel


def main_kernel(
    x_hbm, s_hbm, w_ref, ya,
    xv, xt, sv, msg, xr, part, other, yl, yp, gl, gr, gp, gz, gf, gm, cacc, cr, vb, gi,
    x_in, s_in, pair_send, pair_recv, x_send, x_recv, y_send, y_recv, half_send, half_recv, own_sem,
    g_send, g_recv, gz_send, gz_recv, gf_send, gf_recv, c_send, c_recv,
    up_send, up_recv, down_send, down_recv, zd_send, zd_recv, p1_send, p1_recv, p2_send, p2_recv, fwd_send, fwd_recv,
    via_send, via_recv, on_send, gi_send, gi_recv,
):
    me = lax.axis_index("pos")
    core = lax.axis_index("pix")
    my_y, my_z, my_x = me // (NZ * NX), (me // NX) % NZ, me % NX
    my_d = my_y * NX + my_x
    sibling = 1 - core

    def at(y, z, x):
        return y * (NZ * NX) + z * NX + x

    def at_d(d):
        return at(d // NX, my_z, d % NX)

    def other_d(k):
        return lax.rem(my_y + k // NX, NY) * NX + lax.rem(my_x + k % NX, NX)

    def other_z(k):
        return lax.rem(my_z + k, NZ)

    def remote(src, dst, send_sem, recv_sem, pos, to_core):
        return pltpu.make_async_remote_copy(
            src_ref=src, dst_ref=dst, send_sem=send_sem, recv_sem=recv_sem,
            device_id={"pos": pos, "pix": to_core}, device_id_type=MESH,
        )

    def landed(ref, sem):
        remote(ref, ref, own_sem.at[0], sem, me, sibling).wait_recv()

    def left(ref, sem):
        remote(ref, ref, sem, own_sem.at[0], me, sibling).wait_send()

    x_copy_in = pltpu.make_async_copy(x_hbm, xv, x_in)
    x_copy_in.start()
    s_copy_in = pltpu.make_async_copy(s_hbm, sv, s_in)
    s_copy_in.start()

    barrier = pltpu.get_barrier_semaphore()

    def greet(pos, to_core):
        pl.semaphore_signal(barrier, inc=1, device_id={"pos": pos, "pix": to_core}, device_id_type=MESH)

    greet(me, sibling)

    @pl.loop(1, PLANE)
    def _(k):
        greet(at_d(other_d(k)), core)
        greet(at_d(other_d(k)), sibling)

    @pl.loop(1, NZ)
    def _(k):
        greet(at(my_y, other_z(k), my_x), core)

    x_copy_in.wait()

    @pl.loop(0, 32, unroll=4)
    def _(cp):
        low = xv[pl.ds(cp, 64, stride=64), :]
        high = xv[pl.ds(cp + 32, 64, stride=64), :]
        xt[pl.ds(pl.multiple_of(cp * 128, 128), 128), :] = jnp.concatenate([low, high], axis=0).T

    s_copy_in.wait()
    pl.semaphore_wait(barrier, 1 + 2 * (PLANE - 1) + NZ - 1)

    def x_copy(k, wave):
        d = other_d(k)
        if k in TIES:
            rows = pl.ds(0, 3) if wave == 0 else pl.ds(7, 1)
        else:
            rows = pl.ds(0, 5) if wave == 0 else pl.ds(5, 3)
        return remote(msg.at[d, rows], xr.at[my_d, rows], x_send, x_recv.at[wave], at_d(d), core)

    def via(k):
        return 3 if k // NX == 2 else k // NX, 3 if k % NX == 2 else k % NX

    def via_copy(n):
        k = TIES[n]
        vy, vx = via(k)
        pos = at(lax.rem(my_y + vy, NY), my_z, lax.rem(my_x + vx, NX))
        return remote(msg.at[other_d(k), pl.ds(3, 4)], vb.at[n], via_send, via_recv.at[n], pos, core)

    def on_copy(n, wave):
        k = TIES[n]
        vy, vx = via(k)
        from_d = lax.rem(my_y + NY - vy, NY) * NX + lax.rem(my_x + NX - vx, NX)
        pos = at(lax.rem(my_y + NY + k // NX - vy, NY), my_z, lax.rem(my_x + NX + k % NX - vx, NX))
        src, dst = vb.at[n, pl.ds(2 * wave, 2)], xr.at[from_d, pl.ds(3 + 2 * wave, 2)]
        return remote(src, dst, on_send, x_recv.at[wave], pos, core)

    total = jnp.zeros((64, RANK), jnp.float32)
    for k in TIES + EARLY + LATE + [0]:
        d = other_d(k)
        rows = [xt[pl.ds(at(d // NX, zz, d % NX), 32, stride=128), :] for zz in range(NZ)]
        for zz in range(NZ):
            msg[d, pl.ds(lax.rem(zz + 2 * NZ - 2 - my_z, NZ), 1)] = rows[zz].reshape(1, 32, 128)
        if k in TIES:
            via_copy(TIES.index(k)).start()
        if k in EARLY:
            x_copy(k, 0).start()
            x_copy(k, 1).start()
        xb = jnp.concatenate(rows, axis=0).T.astype(jnp.bfloat16)
        low = sv[d // NX, :, d % NX, 0:32, :].reshape(256, RANK)
        high = sv[d // NX, :, d % NX, 32:64, :].reshape(256, RANK)
        total = total + nn(xb[0:64], low) + nn(xb[64:128], high)
    part[...] = total
    pair = remote(part, other, pair_send, pair_recv, me, sibling)
    pair.start()
    xr[pl.ds(my_d, 1)] = msg[pl.ds(my_d, 1)]
    pair.wait()
    yl[...] = part[...] + other[...]
    my_half = pl.ds(pl.multiple_of(core * 32, 32), 32)
    yp[pl.ds(core, 1), pl.ds(my_d, 1)] = yl[my_half, :].reshape(1, 1, 32, RANK)
    gl[...] = tn(yl[...], yl[...], HIGHEST)

    def g_copy(k):
        d = other_d(k)
        rows = pl.ds(pl.multiple_of(core * 128 + d * 8, 8), 8)
        return remote(gl.at[rows, :], gr.at[my_d], g_send, g_recv, at_d(d), core)

    def gz_copy(k):
        z = other_z(k)
        return remote(gp, gz.at[my_z], gz_send, gz_recv, at(my_y, z, my_x), core)

    my_rows = pl.ds(pl.multiple_of((core * PLANE + my_d) * 8, 8), 8)

    def gf_copy(d, q):
        return remote(gf, gm.at[my_rows, :], gf_send, gf_recv, at_d(d), q)

    def y_copy(k):
        d = other_d(k)
        return remote(yl.at[my_half, :], yp.at[core, my_d], y_send, y_recv, at_d(d), core)

    half_copy = remote(yp.at[core], yp.at[core], half_send, half_recv, me, sibling)

    def own_copy(q):
        return pltpu.make_async_copy(yp.at[q], ya.at[0, q], own_sem.at[q])

    above, below = at(my_y, other_z(1), my_x), at(my_y, other_z(NZ - 1), my_x)

    def up_copy(r):
        src = yp.at[0] if r == 0 else ya.at[NZ - r, 0]
        dst = ya.at[NZ - 1 - r, 0]
        if r == 3:
            src, dst = src.at[pl.ds(0, 8)], dst.at[pl.ds(0, 8)]
        return remote(src, dst, up_send.at[r], up_recv.at[r], above, 0)

    def down_copy(r):
        src = yp.at[0] if r == 0 else ya.at[r, 0]
        dst = ya.at[1 + r, 0]
        if r == 3:
            src, dst = src.at[pl.ds(8, 8)], dst.at[pl.ds(8, 8)]
        return remote(src, dst, down_send.at[r], down_recv.at[r], below, 0)

    def forward(ref):
        remote(ref, ref, fwd_send, fwd_recv, me, sibling).start()

    def zd_copy(k):
        return remote(
            yl.at[my_half, :], ya.at[NZ - k, 1, my_d], zd_send, zd_recv, at(my_y, other_z(k), my_x), 1
        )

    near, far = pl.ds(1, 4), pl.ds(5, 3)

    upper, lower = pl.ds(0, 16), pl.ds(16, 16)

    def x_next(i):
        return lax.rem(my_x + i, NX)

    def y_next(i):
        return lax.rem(my_y + i, NY)

    def p1_copies(t):
        copies = []
        for q, (rel, block, along) in enumerate((
            (near, lambda i: my_y * NX + x_next(i), lambda i: at(my_y, my_z, x_next(i))),
            (far, lambda i: y_next(i) * NX + my_x, lambda i: at(y_next(i), my_z, my_x)),
        )):
            if t == 0:
                up, down = ya.at[rel, 1, block(0)], ya.at[rel, 1, block(0)]
            else:
                up, down = ya.at[rel, 1, block(3), upper], ya.at[rel, 1, block(1), lower]
            copies.append(remote(up, up, p1_send.at[t, q], p1_recv.at[t, q], along(1), 1))
            copies.append(remote(down, down, p1_send.at[t, q], p1_recv.at[t, q], along(3), 1))
        return copies

    def p2_copies(t):
        def row(i):
            return pl.ds(pl.multiple_of(y_next(i) * NX, NX), NX)

        copies = []
        if t == 0:
            up, down = ya.at[near, 1, row(0)], ya.at[near, 1, row(0)]
        else:
            up, down = ya.at[near, 1, row(3), upper], ya.at[near, 1, row(1), lower]
        copies.append(remote(up, up, p2_send.at[t, 0], p2_recv.at[t, 0], at(y_next(1), my_z, my_x), 1))
        copies.append(remote(down, down, p2_send.at[t, 0], p2_recv.at[t, 0], at(y_next(3), my_z, my_x), 1))
        for v in range(NY):
            if t == 0:
                up, down = ya.at[far, 1, v * NX + my_x], ya.at[far, 1, v * NX + my_x]
            else:
                up, down = ya.at[far, 1, v * NX + x_next(3), upper], ya.at[far, 1, v * NX + x_next(1), lower]
            copies.append(remote(up, up, p2_send.at[t, 1], p2_recv.at[t, 1], at(my_y, my_z, x_next(1)), 1))
            copies.append(remote(down, down, p2_send.at[t, 1], p2_recv.at[t, 1], at(my_y, my_z, x_next(3)), 1))
        return copies

    def p_forward(i):
        forward(ya.at[near, 1, pl.ds(pl.multiple_of(y_next(i) * NX, NX), NX)])
        for v in range(NY):
            forward(ya.at[far, 1, v * NX + x_next(i)])

    def p_size(phase, t):
        blocks = (1 if phase == 1 else 4) * (2 if t == 0 else 1)
        return [ya.at[near, 1, pl.ds(0, blocks)], ya.at[far, 1, pl.ds(0, blocks)]]

    def p_landed(phase, t):
        for q in range(2):
            landed(p_size(phase, t)[q], (p1_recv if phase == 1 else p2_recv).at[t, q])

    def p_start(phase, t):
        for copy in (p1_copies if phase == 1 else p2_copies)(t):
            copy.start()

    @pl.loop(1, PLANE)
    def _(k):
        g_copy(k).start()

    @pl.loop(1, PLANE)
    def _(k):
        y_copy(k).start()

    gr[pl.ds(my_d, 1)] = gl[my_rows, :].reshape(1, 8, RANK)

    @pl.when(core == 1)
    def _():
        @pl.loop(1, NZ)
        def _(k):
            zd_copy(k).start()

    landed(gr.at[pl.ds(0, PLANE - 1)], g_recv)
    gp[...] = jnp.sum(gr[...], axis=0)

    @pl.loop(1, NZ)
    def _(k):
        gz_copy(k).start()

    gz[pl.ds(my_z, 1)] = gp[...].reshape(1, 8, RANK)
    landed(gz.at[pl.ds(0, NZ - 1)], gz_recv)
    gf[...] = jnp.sum(gz[...], axis=0)

    @pl.when(core == 0)
    def _():
        gf_copy(my_d, 1).start()

    @pl.loop(1, PLANE)
    def _(k):
        gf_copy(other_d(k), 1).start()

    gm[my_rows, :] = gf[...]
    landed(yp.at[core, pl.ds(0, PLANE - 1)], y_recv)
    half_copy.start()
    own_copy(core).start()

    @pl.when(core == 0)
    def _():
        up_copy(0).start()
        down_copy(0).start()

    @pl.when(core == 1)
    def _():
        landed(ya.at[pl.ds(1, NZ - 1), 1, my_d], zd_recv)
        p_start(1, 0)

    def frames_on(wave):
        for k in LATE:
            x_copy(k, wave).start()
        for n in range(len(TIES)):
            if wave == 0:
                landed(vb.at[n], via_recv.at[n])
            on_copy(n, wave).start()
        for k in TIES:
            x_copy(k, wave).start()

    def ring_landed(r):
        if r < 3:
            landed(ya.at[NZ - 1 - r, 0], up_recv.at[r])
            landed(ya.at[1 + r, 0], down_recv.at[r])
        else:
            landed(ya.at[4, 0, pl.ds(0, 8)], up_recv.at[r])
            landed(ya.at[4, 0, pl.ds(8, 8)], down_recv.at[r])

    def ring_round(r):
        ring_landed(r - 1)
        up_copy(r).start()
        down_copy(r).start()
        forward(ya.at[NZ - r, 0])
        forward(ya.at[r, 0])

    def c_block(s, way):
        return pl.ds((2 - s if way == 0 else 2 + s) % NZ if s < 3 else (7 if way == 0 else 5), 1)

    def c_rows(s, way):
        return pl.ds(0, 32) if s else pl.ds(16 * way, 16)

    def c_copy(s, way):
        src, dst = cacc.at[c_block(s, way), c_rows(s, way)], cr.at[way, pl.ds(s, 1), c_rows(s, way)]
        return remote(src, dst, c_send.at[way, s], c_recv.at[way, s], above if way == 0 else below, core)

    def c_landed(s, way):
        landed(cr.at[way, pl.ds(s, 1), c_rows(s, way)], c_recv.at[way, s])

    def c_step(s):
        for way in range(2):
            if s:
                c_landed(s - 1, way)
                rows = c_rows(s - 1, way)
                cacc[c_block(s, way), rows] += cr[way, pl.ds(s - 1, 1), rows]
            c_copy(s, way).start()

    def coefficients(rows):
        ks = range(PLANE)
        total = jnp.zeros((rows.size * 32, 2 * RANK), jnp.float32)
        zero = jnp.zeros((64, RANK), jnp.float32)
        for n in range(0, len(ks), 2):
            lhs, rhs = [], []
            for k in ks[n : n + 2]:
                d = other_d(k)
                y = jnp.concatenate([yp[0, d], yp[1, d]], axis=0)
                lhs.append(xr[d, rows].reshape(rows.size * 32, 128))
                rhs.append(jnp.concatenate([y, zero], axis=1))
                rhs.append(jnp.concatenate([zero, y], axis=1))
            ah, al = halves(jnp.concatenate(lhs, axis=1))
            bh, bl = halves(jnp.concatenate(rhs, axis=0))
            total = total + (nn(ah, bh) + nn(ah, bl) + nn(al, bh))
        cacc[rows] = total.reshape(rows.size, 32, 2 * RANK)

    def first_sums():
        landed(yp.at[sibling], half_recv)
        own_copy(sibling).start()
        landed(xr.at[pl.ds(0, PLANE - 1), pl.ds(0, 5)], x_recv.at[0])
        coefficients(pl.ds(0, 5))
        c_step(0)

    def second_sums():
        landed(xr.at[pl.ds(0, PLANE - 1), pl.ds(0, 3)], x_recv.at[1])
        coefficients(pl.ds(5, 3))
        c_step(3)

    def step(o, last):
        @pl.when(o == 1)
        def _():
            p_landed(1, 1)
            p_start(2, 0)
            frames_on(1)
            p_forward(0)

        @pl.when(o == 4)
        def _():
            first_sums()

        @pl.when(o == 6)
        def _():
            c_step(1)
            p_landed(2, 0)
            p_start(2, 1)
            p_forward(1)
            p_forward(3)

        @pl.when(o == 7)
        def _():
            c_step(2)

        return factor_step(o, last, gm)

    @pl.when(core == 0)
    def _():
        frames_on(0)
        frames_on(1)
        ring_round(1)
        ring_round(2)
        first_sums()
        c_step(1)
        ring_round(3)
        c_step(2)
        second_sums()
        landed(gi, gi_recv)

    gi_copy = remote(gi, gi, gi_send, gi_recv, me, 0)

    @pl.when(core == 1)
    def _():
        p_landed(1, 0)
        p_start(1, 1)
        frames_on(0)
        landed(gm.at[pl.ds(0, RANK - 8), :], gf_recv)
        panels = RANK // PANEL
        gm[RANK - PANEL : RANK, :] = lax.fori_loop(0, panels, step, jnp.zeros((PANEL, RANK), jnp.float32))
        row_at = lax.broadcasted_iota(jnp.int32, (RANK, RANK), 0)
        lane_at = lax.broadcasted_iota(jnp.int32, (RANK, RANK), 1)
        factor = jnp.where(lane_at <= row_at, gm[...], 0.0)
        gi[...] = tn(factor, factor, HIGHEST)
        gi_copy.start()
        second_sums()

    c_landed(3, 0)
    c_landed(3, 1)
    c = cacc[6] + (cr[0, 3] + cr[1, 3])
    c = jnp.concatenate([c[:, 0:RANK], c[:, RANK:]], axis=0)
    w_ref[...] = nn(c, gi[...], HIGHEST)

    @pl.when(core == 0)
    def _():
        ring_landed(3)
        forward(ya.at[4, 0])

    @pl.when(core == 1)
    def _():
        p_landed(2, 1)
        p_forward(2)

    landed(ya.at[pl.ds(1, NZ - 1), sibling], fwd_recv)
    left(ya.at[pl.ds(1, NZ - 1), core], fwd_send)
    left(gz.at[pl.ds(0, NZ - 1)], gz_send)
    for s in range(4):
        c_copy(s, 0).wait_send()
        c_copy(s, 1).wait_send()
    left(yp.at[core], half_send)
    own_copy(0).wait()
    own_copy(1).wait()
    left(gr.at[pl.ds(0, PLANE - 1)], gf_send)
    left(gr.at[pl.ds(0, PLANE - 1)], g_send)
    left(yp.at[core, pl.ds(0, PLANE - 1)], y_send)
    left(vb, via_send)
    left(vb, on_send)
    left(xr.at[pl.ds(0, len(EARLY + LATE))], x_send)
    left(vb, x_send)

    @pl.when(core == 0)
    def _():
        gf_copy(my_d, 1).wait_send()
        for r in range(4):
            up_copy(r).wait_send()
            down_copy(r).wait_send()

    @pl.when(core == 1)
    def _():
        gi_copy.wait_send()
        left(ya.at[pl.ds(1, NZ - 1), 1, my_d], zd_send)
        for t in range(2):
            for q in range(2):
                left(p_size(1, t)[q], p1_send.at[t, q])
                left(p_size(2, t)[q], p2_send.at[t, q])


def rebuild_kernel(w_ref, y_ref, out_ref):
    my_z = (lax.axis_index("pos") // NX) % NZ
    wh, wl = halves(w_ref[...])
    both = jnp.concatenate([wh, wl], axis=0)
    for rel in range(NZ):
        yh, yl = halves(jnp.concatenate([y_ref[rel, q, x] for x in range(NX) for q in range(2)], axis=0))
        two = nt(both, yh)
        z = lax.rem(my_z + rel, NZ)
        lanes = pl.ds(pl.multiple_of(z * 64 * NX, 64 * NX), 64 * NX)
        out_ref[0, :, lanes] = two[0:64] + (two[64:128] + nt(wh, yl))


VMEM = pl.BlockSpec(memory_space=pltpu.VMEM)
ANY = pl.BlockSpec(memory_space=pl.ANY)
DMA = pltpu.SemaphoreType.DMA


def body(frames, sketch):
    x = frames.transpose(0, 2, 1).reshape(64 * 64, 128)
    s = sketch.reshape(NY, NZ, NX, 64, RANK)
    f32 = jnp.float32
    w, y_all = pl.pallas_call(
        main_kernel,
        out_shape=[
            jax.ShapeDtypeStruct((64, RANK), f32),
            jax.ShapeDtypeStruct((NZ, 2, PLANE, 32, RANK), f32),
        ],
        in_specs=[ANY, ANY],
        out_specs=[VMEM, ANY],
        scratch_shapes=[
            pltpu.VMEM((4096, 128), f32),
            pltpu.VMEM((4096, 128), f32),
            pltpu.VMEM((NY, NZ, NX, 64, RANK), jnp.bfloat16),
            pltpu.VMEM((PLANE, NZ, 32, 128), f32),
            pltpu.VMEM((PLANE, NZ, 32, 128), f32),
            pltpu.VMEM((64, RANK), f32),
            pltpu.VMEM((64, RANK), f32),
            pltpu.VMEM((64, RANK), f32),
            pltpu.VMEM((2, PLANE, 32, RANK), f32),
            pltpu.VMEM((RANK, RANK), f32),
            pltpu.VMEM((PLANE, 8, RANK), f32),
            pltpu.VMEM((8, RANK), f32),
            pltpu.VMEM((NZ, 8, RANK), f32),
            pltpu.VMEM((8, RANK), f32),
            pltpu.VMEM((RANK, RANK), f32),
            pltpu.VMEM((NZ, 32, 2 * RANK), f32),
            pltpu.VMEM((2, 4, 32, 2 * RANK), f32),
            pltpu.VMEM((len(TIES), 4, 32, 128), f32),
            pltpu.VMEM((RANK, RANK), f32),
            DMA, DMA, DMA, DMA,
            DMA, DMA((2,)), DMA, DMA, DMA, DMA, DMA((2,)),
            DMA, DMA, DMA, DMA, DMA, DMA, DMA((2, 4)), DMA((2, 4)),
            DMA((4,)), DMA((4,)), DMA((4,)), DMA((4,)),
            DMA, DMA, DMA((2, 2)), DMA((2, 2)), DMA((2, 2)), DMA((2, 2)), DMA, DMA,
            DMA, DMA((len(TIES),)), DMA, DMA, DMA,
        ],
        compiler_params=pltpu.CompilerParams(collective_id=0, has_side_effects=True, vmem_limit_bytes=58 << 20),
        cost_estimate=pl.CostEstimate(flops=4 * 10**9, bytes_accessed=3 * 10**7, transcendentals=0),
    )(x, s)
    y_all = y_all.reshape(NZ, 2, NY, NX, 32, RANK)
    return pl.pallas_call(
        rebuild_kernel,
        out_shape=jax.ShapeDtypeStruct((1, 64, 8192), f32),
        grid=(NY,),
        in_specs=[
            pl.BlockSpec((64, RANK), lambda i: (0, 0)),
            pl.BlockSpec((NZ, 2, None, NX, 32, RANK), lambda i: (0, 0, i, 0, 0, 0)),
        ],
        out_specs=pl.BlockSpec((1, 64, 2048), lambda i: (0, 0, i)),
        compiler_params=pltpu.CompilerParams(vmem_limit_bytes=58 << 20),
    )(w, y_all)


def solution(mesh):
    in_specs = (P("pos", None, "pix"), P(None, "pix", None))
    out_specs = P("pos", "pix", None)
    return jax.shard_map(body, mesh=mesh, in_specs=in_specs, out_specs=out_specs, check_vma=False)
```

time: 1300 us -> 81 us (0.06)
  waiting for transfers between devices: 1070 us -> 0 us
  Pallas kernels: 0 us -> 80.9 us
  other arithmetic: 74.8 us -> 0 us
  blocking collectives: 56.3 us -> 0 us
  local copies, waits for them, and re-layouts: 45.6 us -> 0 us
  matrix products: 27 us -> 0 us
  between operations: 14.9 us -> 0.01 us
    reduce_scatter x1 -> x0, waiting for transfers between devices: 606 us -> none  [body(): lax.psum_scatter(lax.dot_general(flat_frames, basis_t, (((0,), (1,)), (()...]
    psum x2 -> x0, waiting for transfers between devices: 238 us -> none  [the longest x1 206 us: body(): gram = lax.psum(gram_part, 'pos')]
    all_gather x1 -> x0, waiting for transfers between devices: 224 us -> none  [body(): lax.all_gather(my_coeffs, 'pos', axis=0, tiled=True)]
    pallas_call x0 -> x2, Pallas kernels: none -> 80.9 us  [the longest x1 74.1 us: body(): pl.pallas_call(main_kernel, out_shape=[jax.ShapeDtypeStruct((64, RANK), f...]
    another operation x9 -> x0, other arithmetic: 64.7 us -> none  [the longest x6 34 us: body(): factor = jnp.linalg.cholesky(gram)]
    all_to_all x1 -> x0, blocking collectives: 56.3 us -> none  [body(): lax.all_to_all(rebuilt, 'pos', split_axis=0, concat_axis=2, tiled=True)]
    dot_general x4 -> x0, matrix products: 25.9 us -> none  [the longest x1 10.5 us: body(): jnp.dot(lax.all_gather(my_coeffs, 'pos', axis=0, tiled=True), basis_t, pr...]
    unnamed x8 -> x0, local copies, waits for them, and re-layouts: 19.3 us -> none
  transfers between devices with their start and end apart: 4 -> 0, of which waited for: 4 -> 0; matrix products, arithmetic and copies ran while one was open for 0% -> 0% of each run, Pallas kernels for 0% -> 0%
where the time goes in v1:
time: 81 us; the launch traced here: 80.9 us
  Pallas kernels  80.9 us (100%)
    pallas_call x1, Pallas kernels, body(): pl.pallas_call(main_kernel, out_shape=[jax.ShapeDtypeStruct((64, RANK), f...  74.1 us
    pallas_call x1, Pallas kernels, body(): pl.pallas_call(rebuild_kernel, out_shape=jax.ShapeDtypeStruct((1, 64, 819...  6.75 us

profile of v1, /device:TPU:3, one launch (start us, length us, event | category | flops | bytes accessed | tf_op | source)
XLA Modules:
  0.0 80.9 jit_solution(5414891062842363182)
XLA Ops:
  0.0 74.1 %shard_map.28 = (f32[64,256]{1,0:T(8,128)}, f32[8,2,16,32,256]{4,3,2,1,0:T(8,128)}) custom-call(f32[4096,128]{1,0:T(8,128)} %bitcast.7, bf16[4,8,4,64,256]{4,3,2,1,0:T(8,128)(2,1)} %bitcast.6), custom_call_target="tpu_custom_call" | custom-call | flops 4000000000 | bytes 30000000 | tf_op jit(solution)/shard_map/pallas_call | solution.py:586
  74.1 6.8 %shard_map.29 = f32[1,64,8192]{2,1,0:T(8,128)} custom-call(f32[64,256]{1,0:T(8,128)} %get-tuple-element.7.w_ref, f32[8,2,4,4,32,256]{5,4,3,2,1,0:T(8,128)} %bitcast.5), custom_call_target="tpu_custom_call" | custom-call | tf_op jit(solution)/shard_map/pallas_call | solution.py:625

commit v2 on v1

--- a/solution.py
+++ b/solution.py
@@ -339,6 +339,8 @@
     def _(k):
         y_copy(k).start()
 
+    for k in LATE:
+        x_copy(k, 0).start()
     gr[pl.ds(my_d, 1)] = gl[my_rows, :].reshape(1, 8, RANK)
 
     @pl.when(core == 1)
@@ -382,8 +384,9 @@
         p_start(1, 0)
 
     def frames_on(wave):
-        for k in LATE:
-            x_copy(k, wave).start()
+        if wave == 1:
+            for k in LATE:
+                x_copy(k, wave).start()
         for n in range(len(TIES)):
             if wave == 0:
                 landed(vb.at[n], via_recv.at[n])
@@ -487,12 +490,12 @@
         frames_on(0)
         frames_on(1)
         ring_round(1)
+        first_sums()
         ring_round(2)
-        first_sums()
         c_step(1)
-        ring_round(3)
         c_step(2)
         second_sums()
+        ring_round(3)
         landed(gi, gi_recv)
 
     gi_copy = remote(gi, gi, gi_send, gi_recv, me, 0)

time: 81 us -> 81.1 us (level)
  no operation moved by 1% of the time
where the time goes in v2:
time: 81.1 us; the launch traced here: 81 us
  Pallas kernels  81 us (100%)
    pallas_call x1, Pallas kernels, body(): pl.pallas_call(main_kernel, out_shape=[jax.ShapeDtypeStruct((64, RANK), f...  74.2 us
    pallas_call x1, Pallas kernels, body(): pl.pallas_call(rebuild_kernel, out_shape=jax.ShapeDtypeStruct((1, 64, 819...  6.74 us

profile of v2, /device:TPU:3, one launch (start us, length us, event | category | flops | bytes accessed | tf_op | source)
XLA Modules:
  0.0 81.0 jit_solution(11094599317970125070)
XLA Ops:
  0.0 74.2 %shard_map.28 = (f32[64,256]{1,0:T(8,128)}, f32[8,2,16,32,256]{4,3,2,1,0:T(8,128)}) custom-call(f32[4096,128]{1,0:T(8,128)} %bitcast.7, bf16[4,8,4,64,256]{4,3,2,1,0:T(8,128)(2,1)} %bitcast.6), custom_call_target="tpu_custom_call" | custom-call | flops 4000000000 | bytes 30000000 | tf_op jit(solution)/shard_map/pallas_call | solution.py:589
  74.2 6.7 %shard_map.29 = f32[1,64,8192]{2,1,0:T(8,128)} custom-call(f32[64,256]{1,0:T(8,128)} %get-tuple-element.7.w_ref, f32[8,2,4,4,32,256]{5,4,3,2,1,0:T(8,128)} %bitcast.5), custom_call_target="tpu_custom_call" | custom-call | tf_op jit(solution)/shard_map/pallas_call | solution.py:628

commit v3 on v2

--- a/solution.py
+++ b/solution.py
@@ -406,6 +406,8 @@
         ring_landed(r - 1)
         up_copy(r).start()
         down_copy(r).start()
+
+    def ring_forward(r):
         forward(ya.at[NZ - r, 0])
         forward(ya.at[r, 0])
 
@@ -488,14 +490,17 @@
     @pl.when(core == 0)
     def _():
         frames_on(0)
+        ring_round(1)
         frames_on(1)
-        ring_round(1)
+        ring_forward(1)
         first_sums()
         ring_round(2)
         c_step(1)
+        ring_forward(2)
         c_step(2)
         second_sums()
         ring_round(3)
+        ring_forward(3)
         landed(gi, gi_recv)
 
     gi_copy = remote(gi, gi, gi_send, gi_recv, me, 0)

time: 81.1 us -> 81.4 us (level)
  no operation moved by 1% of the time
where the time goes in v3:
time: 81.4 us; the launch traced here: 81.3 us
  Pallas kernels  81.3 us (100%)
    pallas_call x1, Pallas kernels, body(): pl.pallas_call(main_kernel, out_shape=[jax.ShapeDtypeStruct((64, RANK), f...  74.5 us
    pallas_call x1, Pallas kernels, body(): pl.pallas_call(rebuild_kernel, out_shape=jax.ShapeDtypeStruct((1, 64, 819...  6.76 us

profile of v3, /device:TPU:3, one launch (start us, length us, event | category | flops | bytes accessed | tf_op | source)
XLA Modules:
  0.0 81.3 jit_solution(4709336407790012109)
XLA Ops:
  0.0 74.5 %shard_map.28 = (f32[64,256]{1,0:T(8,128)}, f32[8,2,16,32,256]{4,3,2,1,0:T(8,128)}) custom-call(f32[4096,128]{1,0:T(8,128)} %bitcast.7, bf16[4,8,4,64,256]{4,3,2,1,0:T(8,128)(2,1)} %bitcast.6), custom_call_target="tpu_custom_call" | custom-call | flops 4000000000 | bytes 30000000 | tf_op jit(solution)/shard_map/pallas_call | solution.py:594
  74.5 6.8 %shard_map.29 = f32[1,64,8192]{2,1,0:T(8,128)} custom-call(f32[64,256]{1,0:T(8,128)} %get-tuple-element.7.w_ref, f32[8,2,4,4,32,256]{5,4,3,2,1,0:T(8,128)} %bitcast.5), custom_call_target="tpu_custom_call" | custom-call | tf_op jit(solution)/shard_map/pallas_call | solution.py:633

commit v4 on v2

--- a/solution.py
+++ b/solution.py
@@ -339,8 +339,6 @@
     def _(k):
         y_copy(k).start()
 
-    for k in LATE:
-        x_copy(k, 0).start()
     gr[pl.ds(my_d, 1)] = gl[my_rows, :].reshape(1, 8, RANK)
 
     @pl.when(core == 1)
@@ -356,6 +354,8 @@
     def _(k):
         gz_copy(k).start()
 
+    for k in LATE:
+        x_copy(k, 0).start()
     gz[pl.ds(my_z, 1)] = gp[...].reshape(1, 8, RANK)
     landed(gz.at[pl.ds(0, NZ - 1)], gz_recv)
     gf[...] = jnp.sum(gz[...], axis=0)

time: 81.1 us -> 81 us (level)
  no operation moved by 1% of the time
where the time goes in v4:
time: 81 us; the launch traced here: 80.9 us
  Pallas kernels  80.9 us (100%)
    pallas_call x1, Pallas kernels, body(): pl.pallas_call(main_kernel, out_shape=[jax.ShapeDtypeStruct((64, RANK), f...  74.1 us
    pallas_call x1, Pallas kernels, body(): pl.pallas_call(rebuild_kernel, out_shape=jax.ShapeDtypeStruct((1, 64, 819...  6.75 us

profile of v4, /device:TPU:3, one launch (start us, length us, event | category | flops | bytes accessed | tf_op | source)
XLA Modules:
  0.0 80.9 jit_solution(13639141600625549708)
XLA Ops:
  0.0 74.1 %shard_map.28 = (f32[64,256]{1,0:T(8,128)}, f32[8,2,16,32,256]{4,3,2,1,0:T(8,128)}) custom-call(f32[4096,128]{1,0:T(8,128)} %bitcast.7, bf16[4,8,4,64,256]{4,3,2,1,0:T(8,128)(2,1)} %bitcast.6), custom_call_target="tpu_custom_call" | custom-call | flops 4000000000 | bytes 30000000 | tf_op jit(solution)/shard_map/pallas_call | solution.py:589
  74.1 6.7 %shard_map.29 = f32[1,64,8192]{2,1,0:T(8,128)} custom-call(f32[64,256]{1,0:T(8,128)} %get-tuple-element.7.w_ref, f32[8,2,4,4,32,256]{5,4,3,2,1,0:T(8,128)} %bitcast.5), custom_call_target="tpu_custom_call" | custom-call | tf_op jit(solution)/shard_map/pallas_call | solution.py:628

commit v5 on v2

--- a/solution.py
+++ b/solution.py
@@ -474,10 +474,6 @@
         @pl.when(o == 6)
         def _():
             c_step(1)
-            p_landed(2, 0)
-            p_start(2, 1)
-            p_forward(1)
-            p_forward(3)
 
         @pl.when(o == 7)
         def _():
@@ -513,6 +509,10 @@
         factor = jnp.where(lane_at <= row_at, gm[...], 0.0)
         gi[...] = tn(factor, factor, HIGHEST)
         gi_copy.start()
+        p_landed(2, 0)
+        p_start(2, 1)
+        p_forward(1)
+        p_forward(3)
         second_sums()
 
     c_landed(3, 0)

time: 81.1 us -> 81.1 us (level)
  no operation moved by 1% of the time
where the time goes in v5:
time: 81.1 us; the launch traced here: 81 us
  Pallas kernels  81 us (100%)
    pallas_call x1, Pallas kernels, body(): pl.pallas_call(main_kernel, out_shape=[jax.ShapeDtypeStruct((64, RANK), f...  74.2 us
    pallas_call x1, Pallas kernels, body(): pl.pallas_call(rebuild_kernel, out_shape=jax.ShapeDtypeStruct((1, 64, 819...  6.74 us

profile of v5, /device:TPU:3, one launch (start us, length us, event | category | flops | bytes accessed | tf_op | source)
XLA Modules:
  0.0 81.0 jit_solution(14303184657491276733)
XLA Ops:
  0.0 74.2 %shard_map.28 = (f32[64,256]{1,0:T(8,128)}, f32[8,2,16,32,256]{4,3,2,1,0:T(8,128)}) custom-call(f32[4096,128]{1,0:T(8,128)} %bitcast.7, bf16[4,8,4,64,256]{4,3,2,1,0:T(8,128)(2,1)} %bitcast.6), custom_call_target="tpu_custom_call" | custom-call | flops 4000000000 | bytes 30000000 | tf_op jit(solution)/shard_map/pallas_call | solution.py:589
  74.2 6.7 %shard_map.29 = f32[1,64,8192]{2,1,0:T(8,128)} custom-call(f32[64,256]{1,0:T(8,128)} %get-tuple-element.7.w_ref, f32[8,2,4,4,32,256]{5,4,3,2,1,0:T(8,128)} %bitcast.5), custom_call_target="tpu_custom_call" | custom-call | tf_op jit(solution)/shard_map/pallas_call | solution.py:628
